TPU v7x, 32 devices: a whole 2x2x4 slice. The times are simulated.
32 devices in a mesh: ctx: 16 (over z, y, x), dp: 2 (over core).
Axes of the slice: x: 2, y: 2, z: 4, core: 2. Of those that a mesh axis runs over, the one named last changes fastest.
Arguments:
- queries: bfloat16 [2048, 2048], P('ctx', 'dp'), may hold values from -192 to 192
- keys: bfloat16 [2048, 128], P('ctx'), may hold values from -32 to 32
- values: bfloat16 [2048, 128], P('ctx'), may hold values from -6 to 6
- out_grads: bfloat16 [2048, 2048], P('ctx', 'dp'), may hold values from -6 to 6
- doc_lengths: int32 [8], replicated, may hold values from 1 to 1152, 2048 in all
Outputs:
- query_grads: bfloat16 [2048, 2048], P('ctx', 'dp')
- key_grads: bfloat16 [2048, 128], P(('ctx', 'dp'))
- value_grads: bfloat16 [2048, 128], P(('ctx', 'dp'))
Inputs may be any that keep to these rules, and one draw needn't show every extreme that they name: `doc_lengths`: document lengths in order of position; they sum to 2048 and the longest document has exactly 1152 tokens.
All inputs are finite; a program needn't handle non-finite values.
Results may differ from a plain program's by a relative error of at most 0.023.
Values may be sent and summed in bfloat16 or wider, within the bound.
No kernel may reach another device: no remote copies, remote signals or barrier semaphores. Data moves between devices by JAX's collectives and lax.ppermute only.
A program may use at most 64 MiB of HBM per device.

v0:
```python
import functools
import math

import jax
import jax.numpy as jnp
from jax import lax
from jax.experimental import pallas as pl
from jax.experimental.pallas import tpu as pltpu
from jax.sharding import PartitionSpec as P

masked_value = -1e30

vmem = pl.BlockSpec(memory_space=pltpu.VMEM)
smem = pl.BlockSpec(memory_space=pltpu.SMEM)
hbm = pl.BlockSpec(memory_space=pltpu.HBM)


def row_position(ctx_index, start, ctx_count, rows, span_rows):
    low = ctx_index * span_rows + start
    high = (2 * ctx_count - 1 - ctx_index) * span_rows + start - span_rows
    return pl.multiple_of(jnp.where(start < span_rows, low, high), rows)


def span_first(half, ctx_count, span_rows):
    ctx_index = lax.axis_index("ctx")
    return (ctx_index if half == 0 else 2 * ctx_count - 1 - ctx_index) * span_rows


def prepare_kernel(
    ctx_count,
    tile,
    lengths_ref,
    q_hbm,
    g_hbm,
    line_ref,
    stack_ref,
    flip_ref,
    starts_ref,
    tiles_ref,
    same_ref,
    raw_ref,
    sems,
):
    tok_rows = q_hbm.shape[0]
    head_width = stack_ref.shape[3]
    cols = stack_ref.shape[2]
    span_rows = tok_rows // 2
    copies = [
        pltpu.make_async_copy(source, raw_ref.at[slot], sems.at[slot])
        for slot, source in enumerate((q_hbm, g_hbm))
    ]
    for copy in copies:
        copy.start()
    same_ref[...] = line_ref[...]
    lane = lax.broadcasted_iota(jnp.int32, tiles_ref.shape, 1)
    tiles = jnp.zeros(tiles_ref.shape, jnp.int32)
    for half in range(2):
        first = span_first(half, ctx_count, span_rows)
        query_pos = first + lax.rem(
            lax.broadcasted_iota(jnp.int32, (1, cols), 1), jnp.int32(span_rows)
        )
        doc_start = jnp.zeros((1, cols), jnp.int32)
        first_key = jnp.int32(0)
        end = jnp.int32(0)
        for doc in range(lengths_ref.shape[0]):
            end = end + lengths_ref[doc]
            doc_start = jnp.where(query_pos >= end, end, doc_start)
            first_key = jnp.where(first >= end, end, first_key)
        starts_ref[half] = doc_start
        count = (first + span_rows - first_key + tile - 1) // tile
        tiles = jnp.where(lane == half, count, tiles)
    tiles_ref[...] = tiles
    for slot, copy in enumerate(copies):
        copy.wait()
        for half in range(2):
            for head in range(q_hbm.shape[1] // head_width):
                stack_ref[half, slot, pl.ds(head * span_rows, span_rows), :] = raw_ref[
                    slot,
                    pl.ds(half * span_rows, span_rows),
                    pl.ds(head * head_width, head_width),
                ]
            flip_ref[half, slot] = stack_ref[half, slot].T


def attend_kernel(
    ctx_count, dp_count, inner, tile, tiles_ref, starts_ref, stack_ref, flip_ref, *refs
):
    outer = ctx_count // inner
    piece_count = dp_count * inner
    kv_refs = refs[:piece_count]
    refs = refs[piece_count:]
    keys_ref, dlogits_ref = refs[:2]
    dkv_refs = refs[2 : piece_count + 2]
    values_ref, acc_ref, terms_ref, dweights_ref, tops_ref, counts_ref, sem = refs[
        piece_count + 2 :
    ]
    cols, head_width = stack_ref.shape[2:]
    tok_rows = (keys_ref.shape[0] - tile) // ctx_count
    part_rows = tok_rows // dp_count
    span_rows = tok_rows // 2
    scale = head_width ** (-0.5)
    ctx_index = lax.axis_index("ctx")
    dp_index = lax.axis_index("dp")
    count_copy = pltpu.make_async_copy(tiles_ref, counts_ref, sem)
    count_copy.start()

    def blocks():
        for piece in range(piece_count):
            for block in range(outer):
                owner = ctx_index ^ (piece % inner) ^ (block * inner)
                first = (dp_index ^ (piece // inner)) * part_rows
                position = row_position(owner, first, ctx_count, part_rows, span_rows)
                yield (
                    piece,
                    pl.ds(block * part_rows, part_rows),
                    pl.ds(tile + position, part_rows),
                )

    dead = jnp.zeros((tile, head_width), jnp.bfloat16)
    keys_ref[:tile, :] = dead
    values_ref[:tile, :] = dead
    for piece, here, ordered in blocks():
        keys_ref[ordered, :] = kv_refs[piece][here, :head_width]
        values_ref[ordered, :] = kv_refs[piece][here, head_width:]
    acc_ref[...] = jnp.zeros_like(acc_ref)
    count_copy.wait()

    for half in range(2):
        first = span_first(half, ctx_count, span_rows)
        query_pos = first + lax.rem(
            lax.broadcasted_iota(jnp.int32, (1, cols), 1), jnp.int32(span_rows)
        )
        doc_start = starts_ref[half]
        count = counts_ref[0, half]

        def tile_rows(index):
            position = first + span_rows - (index + 1) * tile
            rows = pl.ds(pl.multiple_of(tile + position, span_rows), tile)
            return position, rows, pl.ds(pl.multiple_of(index * tile, tile), tile)

        def sums_step(index, state):
            top, total, mixed = state
            position, rows, slot = tile_rows(index)
            logits = jnp.dot(
                keys_ref[rows, :], flip_ref[half, 0], preferred_element_type=jnp.float32
            )
            key_pos = lax.broadcasted_iota(jnp.int32, (tile, cols), 0)
            live = (key_pos >= doc_start - position) & (key_pos <= query_pos - position)
            logits = jnp.where(live, logits * (scale * math.log2(math.e)), masked_value)
            new_top = jnp.maximum(top, jnp.max(logits, axis=0, keepdims=True))
            terms = jnp.exp2(logits - new_top)
            dweights = jnp.dot(
                values_ref[rows, :], flip_ref[half, 1], preferred_element_type=jnp.float32
            )
            terms_ref[slot, :] = terms
            dweights_ref[slot, :] = dweights
            tops_ref[pl.ds(index, 1), :] = new_top
            decay = jnp.exp2(top - new_top)
            return (
                new_top,
                total * decay + jnp.sum(terms, axis=0, keepdims=True),
                mixed * decay + jnp.sum(terms * dweights, axis=0, keepdims=True),
            )

        zero = jnp.zeros((1, cols), jnp.float32)
        top, total, mixed = lax.fori_loop(
            0, count, sums_step, (jnp.full_like(zero, masked_value), zero, zero)
        )
        inverse = 1.0 / total
        delta = mixed * inverse

        def grads_step(index, carry):
            _, rows, slot = tile_rows(index)
            factor = jnp.exp2(tops_ref[pl.ds(index, 1), :] - top) * inverse
            weights = terms_ref[slot, :] * factor
            dlogits = (weights * (dweights_ref[slot, :] - delta)).astype(jnp.bfloat16)
            dlogits_ref[half, slot, :] = dlogits
            acc_ref[1, rows, :] += jnp.dot(
                weights.astype(jnp.bfloat16),
                stack_ref[half, 1],
                preferred_element_type=jnp.float32,
            )
            acc_ref[0, rows, :] += jnp.dot(
                dlogits, stack_ref[half, 0], preferred_element_type=jnp.float32
            )
            return carry

        lax.fori_loop(0, count, grads_step, 0)

    for piece, here, ordered in blocks():
        dkv_refs[piece][here, :head_width] = (scale * acc_ref[0, ordered, :]).astype(jnp.bfloat16)
        dkv_refs[piece][here, head_width:] = acc_ref[1, ordered, :].astype(jnp.bfloat16)


def query_kernel(
    ctx_count,
    tile,
    tiles_ref,
    keys_ref,
    dlogits_ref,
    passed_ref,
    dq_ref,
    same_ref,
    sum_ref,
    counts_ref,
    sem,
):
    tok_rows = dq_ref.shape[0]
    head_width = keys_ref.shape[1]
    span_rows = tok_rows // 2
    scale = head_width ** (-0.5)
    count_copy = pltpu.make_async_copy(tiles_ref, counts_ref, sem)
    count_copy.start()
    same_ref[...] = passed_ref[...]
    count_copy.wait()
    for half in range(2):
        end = span_first(half, ctx_count, span_rows) + span_rows
        sum_ref[...] = jnp.zeros_like(sum_ref)

        def query_step(index, carry):
            rows = pl.ds(pl.multiple_of(end - index * tile, span_rows), tile)
            slot = pl.ds(pl.multiple_of(index * tile, tile), tile)
            sum_ref[...] += jnp.dot(
                keys_ref[rows, :].T, dlogits_ref[half, slot, :], preferred_element_type=jnp.float32
            )
            return carry

        lax.fori_loop(0, counts_ref[0, half], query_step, 0)
        grads = (scale * sum_ref[...]).T.astype(jnp.bfloat16)
        for head in range(dq_ref.shape[1] // head_width):
            dq_ref[
                pl.ds(half * span_rows, span_rows), pl.ds(head * head_width, head_width)
            ] = grads[head * span_rows : (head + 1) * span_rows]


def prepare(ctx_count, tile, doc_lengths, queries, out_grads, head_width, line):
    tok_rows, width = queries.shape
    cols = width // head_width * (tok_rows // 2)
    return pl.pallas_call(
        functools.partial(prepare_kernel, ctx_count, tile),
        out_shape=(
            jax.ShapeDtypeStruct((2, 2, cols, head_width), jnp.bfloat16),
            jax.ShapeDtypeStruct((2, 2, head_width, cols), jnp.bfloat16),
            jax.ShapeDtypeStruct((2, 1, cols), jnp.int32),
            jax.ShapeDtypeStruct((8, 128), jnp.int32),
            jax.ShapeDtypeStruct(line.shape, line.dtype),
        ),
        in_specs=[smem, hbm, hbm, vmem],
        out_specs=[vmem] * 5,
        scratch_shapes=[
            pltpu.VMEM((2, tok_rows, width), jnp.bfloat16),
            pltpu.SemaphoreType.DMA((2,)),
        ],
        compiler_params=pltpu.CompilerParams(vmem_limit_bytes=4 * 1024 * 1024),
    )(doc_lengths, queries, out_grads, line)


def attend(ctx_count, dp_count, inner, tile, tiles, starts, stacked, flipped, pieces):
    cols, head_width = stacked.shape[2:]
    seq = dp_count * inner * pieces[0].shape[0]
    slots = -(-seq // tile)
    results = pl.pallas_call(
        functools.partial(attend_kernel, ctx_count, dp_count, inner, tile),
        out_shape=[
            jax.ShapeDtypeStruct((tile + seq, head_width), jnp.bfloat16),
            jax.ShapeDtypeStruct((2, slots * tile, cols), jnp.bfloat16),
        ]
        + [jax.ShapeDtypeStruct(piece.shape, jnp.bfloat16) for piece in pieces],
        in_specs=[vmem] * (4 + len(pieces)),
        out_specs=[vmem] * (2 + len(pieces)),
        scratch_shapes=[
            pltpu.VMEM((tile + seq, head_width), jnp.bfloat16),
            pltpu.VMEM((2, tile + seq, head_width), jnp.float32),
            pltpu.VMEM((slots * tile, cols), jnp.float32),
            pltpu.VMEM((slots * tile, cols), jnp.float32),
            pltpu.VMEM((slots, cols), jnp.float32),
            pltpu.SMEM((8, 128), jnp.int32),
            pltpu.SemaphoreType.DMA,
        ],
        compiler_params=pltpu.CompilerParams(vmem_limit_bytes=32 * 1024 * 1024),
    )(tiles, starts, stacked, flipped, *pieces)
    return results[0], results[1], results[2:]


def query_side(ctx_count, tile, tiles, keys_ordered, dlogits, passed, tok_rows):
    cols = dlogits.shape[2]
    head_width = keys_ordered.shape[1]
    return pl.pallas_call(
        functools.partial(query_kernel, ctx_count, tile),
        out_shape=(
            jax.ShapeDtypeStruct(
                (tok_rows, cols // (tok_rows // 2) * head_width), jnp.bfloat16
            ),
            jax.ShapeDtypeStruct(passed.shape, passed.dtype),
        ),
        in_specs=[vmem] * 4,
        out_specs=(vmem, vmem),
        scratch_shapes=[
            pltpu.VMEM((head_width, cols), jnp.float32),
            pltpu.SMEM((8, 128), jnp.int32),
            pltpu.SemaphoreType.DMA,
        ],
        compiler_params=pltpu.CompilerParams(vmem_limit_bytes=8 * 1024 * 1024),
    )(tiles, keys_ordered, dlogits, passed)


def swap(value, axis, offset):
    pairs = [(index, index ^ offset) for index in range(lax.axis_size(axis))]
    return lax.ppermute(value, axis, pairs)


def total_of(terms):
    return sum(term.astype(jnp.float32) for term in terms).astype(jnp.bfloat16)


def body(queries, keys, values, out_grads, doc_lengths):
    ctx_count = lax.axis_size("ctx")
    dp_count = lax.axis_size("dp")
    inner = math.gcd(4, ctx_count)
    outer = ctx_count // inner
    tok_rows, head_width = keys.shape
    part_rows = tok_rows // dp_count
    tile = math.gcd(256, ctx_count * tok_rows)
    own = lax.dynamic_slice_in_dim(
        jnp.concatenate([keys, values], axis=1), lax.axis_index("dp") * part_rows, part_rows, 0
    )
    line = jnp.concatenate(
        [own] + [swap(own, "ctx", block * inner) for block in range(1, outer)], axis=0
    )
    plane = [line] + [swap(line, "ctx", offset) for offset in range(1, inner)]
    stacked, flipped, starts, tiles, plane[0] = prepare(
        ctx_count, tile, doc_lengths, queries, out_grads, head_width, line
    )
    pieces = plane + [
        swap(piece, "dp", offset) for offset in range(1, dp_count) for piece in plane
    ]
    keys_ordered, dlogits, parts = attend(
        ctx_count, dp_count, inner, tile, tiles, starts, stacked, flipped, pieces
    )
    plane_sums = [
        total_of(
            [parts[offset]]
            + [swap(parts[far * inner + offset], "dp", far) for far in range(1, dp_count)]
        )
        for offset in range(inner)
    ]
    query_grads, plane_sums[0] = query_side(
        ctx_count, tile, tiles, keys_ordered, dlogits, plane_sums[0], tok_rows
    )
    line_sum = total_of(
        [plane_sums[0]] + [swap(plane_sums[offset], "ctx", offset) for offset in range(1, inner)]
    )
    blocks = jnp.split(line_sum, outer, axis=0)
    kv_grads = total_of(
        [blocks[0]] + [swap(blocks[block], "ctx", block * inner) for block in range(1, outer)]
    )
    return (query_grads, kv_grads[:, :head_width], kv_grads[:, head_width:])


def solution(mesh):
    return jax.shard_map(
        body,
        mesh=mesh,
        in_specs=(P("ctx", "dp"), P("ctx", None), P("ctx", None), P("ctx", "dp"), P()),
        out_specs=(P("ctx", "dp"), P(("ctx", "dp"), None), P(("ctx", "dp"), None)),
        check_vma=False,
    )
```

profile of v0, /device:TPU:0, one launch (start us, length us, event | category | flops | bytes accessed | tf_op | source)
XLA Modules:
  0.0 46.6 jit_solution(5060298120374976789)
XLA Ops:
  0.6 0.7 %fusion = bf16[64,256]{1,0:T(8,128)(2,1)S(1)} fusion(s32[]{:T(128)S(6)} %select_n.3, bf16[128,128]{1,0:T(8,128)(2,1)} %param.6, bf16[128,128]{1,0:T(8,128)(2,1)} %param.7), kind=kLoop, calls=%fused_computation.9 | loop fusion | flops 65536 | bytes 98308 | tf_op jit(solution)/shard_map/concatenate | solution.py:325
  1.4 5.0 %collective-permute-start.2 = (bf16[64,256]{1,0:T(8,128)(2,1)S(1)}, bf16[64,256]{1,0:T(8,128)(2,1)S(1)}, u32[]{:S(2)}, u32[]{:S(2)}) collective-permute-start(bf16[64,256]{1,0:T(8,128)(2,1)S(1)} %fusion), channel_id=1, source_target_pairs={{0,24},{2,26},{4,28},{6,30},{8,16},{10,18},{12,20},{14,22},{16,8},... | collective-permute-start | bytes 98312 | tf_op jit(solution)/shard_map/ppermute | solution.py:309
  6.4 0.6 %collective-permute-start = (bf16[64,256]{1,0:T(8,128)(2,1)S(1)}, bf16[64,256]{1,0:T(8,128)(2,1)S(1)}, u32[]{:S(2)}, u32[]{:S(2)}) collective-permute-start(bf16[64,256]{1,0:T(8,128)(2,1)S(1)} %fusion), channel_id=1, source_target_pairs={{0,8},{2,10},{4,12},{6,14},{8,0},{10,2},{12,4},{14,6},{16,24},{18,... | collective-permute-start | bytes 98312 | tf_op jit(solution)/shard_map/ppermute | solution.py:309
  7.1 1.3 %collective-permute-done.2 = bf16[64,256]{1,0:T(8,128)(2,1)S(1)} collective-permute-done((bf16[64,256]{1,0:T(8,128)(2,1)S(1)}, bf16[64,256]{1,0:T(8,128)(2,1)S(1)}, u32[]{:S(2)}, u32[]{:S(2)}) %collective-permute-start.2) | collective-permute-done | bytes 32800 | tf_op jit(solution)/shard_map/ppermute | solution.py:309
  8.3 2.9 %collective-permute-done.1 = bf16[64,256]{1,0:T(8,128)(2,1)S(1)} collective-permute-done((bf16[64,256]{1,0:T(8,128)(2,1)S(1)}, bf16[64,256]{1,0:T(8,128)(2,1)S(1)}, u32[]{:S(2)}, u32[]{:S(2)}) %collective-permute-start.1) | collective-permute-done | bytes 32800 | tf_op jit(solution)/shard_map/ppermute | solution.py:309
  11.3 2.5 %collective-permute-start.5 = (bf16[256,256]{1,0:T(8,128)(2,1)S(1)}, bf16[256,256]{1,0:T(8,128)(2,1)S(1)}, u32[]{:S(2)}, u32[]{:S(2)}) collective-permute-start(bf16[256,256]{1,0:T(8,128)(2,1)S(1)} %pad_maximum_fusion.line_ref), channel_id=1, source_target_pairs={{0,6},{2,4},{4,2},{6,0},{8,14},{10,12},{12,10},{14,8},{16,22},{18,... | collective-permute-start | bytes 393224 | tf_op jit(solution)/shard_map/ppermute | solution.py:309
  14.3 0.5 %collective-permute-start.3 = (bf16[256,256]{1,0:T(8,128)(2,1)S(1)}, bf16[256,256]{1,0:T(8,128)(2,1)S(1)}, u32[]{:S(2)}, u32[]{:S(2)}) collective-permute-start(bf16[256,256]{1,0:T(8,128)(2,1)S(1)} %pad_maximum_fusion.line_ref), channel_id=1, source_target_pairs={{0,2},{2,0},{4,6},{6,4},{8,10},{10,8},{12,14},{14,12},{16,18},{18,... | collective-permute-start | bytes 393224 | tf_op jit(solution)/shard_map/ppermute | solution.py:309
  14.8 0.9 %copy-done = bf16[128,1024]{1,0:T(8,128)(2,1)S(1)} copy-done((bf16[128,1024]{1,0:T(8,128)(2,1)S(1)}, bf16[128,1024]{1,0:T(8,128)(2,1)}, u32[]{:S(2)}) %copy-start) | copy-done | bytes 262168
  15.8 0.9 %copy-done.1 = bf16[128,1024]{1,0:T(8,128)(2,1)S(1)} copy-done((bf16[128,1024]{1,0:T(8,128)(2,1)S(1)}, bf16[128,1024]{1,0:T(8,128)(2,1)}, u32[]{:S(2)}) %copy-start.1) | copy-done | bytes 262168
  16.7 0.7 %copy-done.2 = s32[8]{0:T(128)S(1)} copy-done((s32[8]{0:T(128)S(1)}, s32[8]{0:T(128)}, u32[]{:S(2)}) %copy-start.2) | copy-done | bytes 56
  17.4 0.9 %shard_map.76 = (bf16[2,2,512,128]{3,2,1,0:T(8,128)(2,1)S(1)}, bf16[2,2,128,512]{3,2,1,0:T(8,128)(2,1)S(1)}, s32[2,1,512]{2,1,0:T(1,128)S(1)}, s32[8,128]{1,0:T(8,128)S(1)}, bf16[256,256]{1,0:T(8,128)(2,1)S(1)}) custom-call(s32[8]{0:T(128)S(1)} %copy-done.2, bf16[128,1024]{1,0:T(8,128)(2,1)S(1)} %copy-done, bf16[128,1024]{1,0:T(8,128)(2,1)S(1)} %copy-done.1, ...), custom_call_target="tpu_custom_call" | custom-call | tf_op jit(solution)/shard_map/pallas_call | solution.py:239
  19.9 0.8 %collective-permute-done.8.refs_6_ = bf16[256,256]{1,0:T(8,128)(2,1)S(1)} collective-permute-done((bf16[256,256]{1,0:T(8,128)(2,1)S(1)}, bf16[256,256]{1,0:T(8,128)(2,1)S(1)}, u32[]{:S(2)}, u32[]{:S(2)}) %collective-permute-start.8) | collective-permute-done | bytes 131104 | tf_op jit(solution)/shard_map/ppermute | solution.py:309
  20.9 2.6 %shard_map.77 = (bf16[2304,128]{1,0:T(8,128)(2,1)S(1)}, bf16[2,2048,512]{2,1,0:T(8,128)(2,1)S(1)}, bf16[256,256]{1,0:T(8,128)(2,1)S(1)}, bf16[256,256]{1,0:T(8,1...) custom-call(s32[8,128]{1,0:T(8,128)S(1)} %get-tuple-element.20.tiles, ...), custom_call_target="tpu_custom_call" | custom-call | tf_op jit(solution)/shard_map/pallas_call | solution.py:262
  25.0 1.1 %collective-permute-start.12 = (bf16[256,256]{1,0:T(8,128)(2,1)S(1)}, bf16[256,256]{1,0:T(8,128)(2,1)S(1)}, u32[]{:S(2)}, u32[]{:S(2)}) collective-permute-start(bf16[256,256]{1,0:T(8,128)(2,1)S(1)} %add_convert_fusion.3), channel_id=1, source_target_pairs={{0,2},{2,0},{4,6},{6,4},{8,10},{10,8},{12,14},{14,12},{16,18},{18,... | collective-permute-start | bytes 393224 | tf_op jit(solution)/shard_map/ppermute | solution.py:309
  26.1 1.6 %collective-permute-start.14 = (bf16[256,256]{1,0:T(8,128)(2,1)S(1)}, bf16[256,256]{1,0:T(8,128)(2,1)S(1)}, u32[]{:S(2)}, u32[]{:S(2)}) collective-permute-start(bf16[256,256]{1,0:T(8,128)(2,1)S(1)} %add_convert_fusion.2), channel_id=1, source_target_pairs={{0,4},{2,6},{4,0},{6,2},{8,12},{10,14},{12,8},{14,10},{16,20},{18,... | collective-permute-start | bytes 393224 | tf_op jit(solution)/shard_map/ppermute | solution.py:309
  27.7 1.0 %collective-permute-start.16 = (bf16[256,256]{1,0:T(8,128)(2,1)S(1)}, bf16[256,256]{1,0:T(8,128)(2,1)S(1)}, u32[]{:S(2)}, u32[]{:S(2)}) collective-permute-start(bf16[256,256]{1,0:T(8,128)(2,1)S(1)} %add_convert_fusion.1), channel_id=1, source_target_pairs={{0,6},{2,4},{4,2},{6,0},{8,14},{10,12},{12,10},{14,8},{16,22},{18,... | collective-permute-start | bytes 393224 | tf_op jit(solution)/shard_map/ppermute | solution.py:309
  28.8 2.0 %shard_map.78 = (bf16[128,1024]{1,0:T(8,128)(2,1)}, bf16[256,256]{1,0:T(8,128)(2,1)S(1)}) custom-call(s32[8,128]{1,0:T(8,128)S(1)} %get-tuple-element.20.tiles_ref, bf16[2304,128]{1,0:T(8,128)(2,1)S(1)} %get-tuple-element.25.keys_ref, bf16[2,2048,512]{2,1,0:T(8,128)(2,1)S(1)} %get-tuple-element.26.dlogits_ref, bf16[256,256]{1,0:T(8,128)(2,1)S(1)} %add_convert_fusion.4.passed_ref), custom_call_target="tpu_custom_call" | custom-call | tf_op jit(solution)/shard_map/pallas_call | solution.py:288
  30.8 0.6 %collective-permute-done.12 = bf16[256,256]{1,0:T(8,128)(2,1)S(1)} collective-permute-done((bf16[256,256]{1,0:T(8,128)(2,1)S(1)}, bf16[256,256]{1,0:T(8,128)(2,1)S(1)}, u32[]{:S(2)}, u32[]{:S(2)}) %collective-permute-start.12) | collective-permute-done | bytes 131104 | tf_op jit(solution)/shard_map/ppermute | solution.py:309
  31.4 3.1 %collective-permute-done.14 = bf16[256,256]{1,0:T(8,128)(2,1)S(1)} collective-permute-done((bf16[256,256]{1,0:T(8,128)(2,1)S(1)}, bf16[256,256]{1,0:T(8,128)(2,1)S(1)}, u32[]{:S(2)}, u32[]{:S(2)}) %collective-permute-start.14) | collective-permute-done | bytes 131104 | tf_op jit(solution)/shard_map/ppermute | solution.py:309
  34.5 0.8 %collective-permute-start.17 = (bf16[64,256]{1,0:T(8,128)(2,1)S(1)}, bf16[64,256]{1,0:T(8,128)(2,1)S(1)}, u32[]{:S(2)}, u32[]{:S(2)}) collective-permute-start(bf16[64,256]{1,0:T(8,128)(2,1)S(1)} %get-tuple-element.37), channel_id=1, source_target_pairs={{0,8},{2,10},{4,12},{6,14},{8,0},{10,2},{12,4},{14,6},{16,24},{18,... | collective-permute-start | bytes 98312 | tf_op jit(solution)/shard_map/ppermute | solution.py:309
  35.3 5.8 %collective-permute-start.19 = (bf16[64,256]{1,0:T(8,128)(2,1)S(1)}, bf16[64,256]{1,0:T(8,128)(2,1)S(1)}, u32[]{:S(2)}, u32[]{:S(2)}) collective-permute-start(bf16[64,256]{1,0:T(8,128)(2,1)S(1)} %get-tuple-element.38), channel_id=1, source_target_pairs={{0,24},{2,26},{4,28},{6,30},{8,16},{10,18},{12,20},{14,22},{16,8},... | collective-permute-start | bytes 98312 | tf_op jit(solution)/shard_map/ppermute | solution.py:309
  41.6 1.7 %collective-permute-done.19 = bf16[64,256]{1,0:T(8,128)(2,1)S(1)} collective-permute-done((bf16[64,256]{1,0:T(8,128)(2,1)S(1)}, bf16[64,256]{1,0:T(8,128)(2,1)S(1)}, u32[]{:S(2)}, u32[]{:S(2)}) %collective-permute-start.19) | collective-permute-done | bytes 32800 | tf_op jit(solution)/shard_map/ppermute | solution.py:309
  43.3 2.6 %collective-permute-done.18 = bf16[64,256]{1,0:T(8,128)(2,1)S(1)} collective-permute-done((bf16[64,256]{1,0:T(8,128)(2,1)S(1)}, bf16[64,256]{1,0:T(8,128)(2,1)S(1)}, u32[]{:S(2)}, u32[]{:S(2)}) %collective-permute-start.18) | collective-permute-done | bytes 32800 | tf_op jit(solution)/shard_map/ppermute | solution.py:309
  45.9 0.6 %fusion.2 = (bf16[64,128]{1,0:T(8,128)(2,1)}, bf16[64,128]{1,0:T(8,128)(2,1)}) fusion(bf16[64,256]{1,0:T(8,128)(2,1)S(1)} %add_convert_fusion.5), kind=kLoop, calls=%fused_computation.11 | loop fusion | bytes 65536 | tf_op jit(solution)/shard_map/slice | solution.py:357
  (35 shorter events, 4.5 us)
Async XLA Ops:
  1.4 6.9 %collective-permute-start.2 = (bf16[64,256]{1,0:T(8,128)(2,1)S(1)}, bf16[64,256]{1,0:T(8,128)(2,1)S(1)}, u32[]{:S(2)}, u32[]{:S(2)}) collective-permute-start(bf16[64,256]{1,0:T(8,128)(2,1)S(1)} %fusion), channel_id=1, source_target_pairs={{0,24},{2,26},{4,28},{6,30},{8,16},{10,18},{12,20},{14,22},{16,8},... | collective-permute-start | bytes 98312 | tf_op jit(solution)/shard_map/ppermute | solution.py:309
  6.4 4.8 %collective-permute-start.1 = (bf16[64,256]{1,0:T(8,128)(2,1)S(1)}, bf16[64,256]{1,0:T(8,128)(2,1)S(1)}, u32[]{:S(2)}, u32[]{:S(2)}) collective-permute-start(bf16[64,256]{1,0:T(8,128)(2,1)S(1)} %fusion), channel_id=1, source_target_pairs={{0,16},{2,18},{4,20},{6,22},{8,24},{10,26},{12,28},{14,30},{16,0},... | collective-permute-start | bytes 98312 | tf_op jit(solution)/shard_map/ppermute | solution.py:309
  6.4 4.8 %collective-permute-start = (bf16[64,256]{1,0:T(8,128)(2,1)S(1)}, bf16[64,256]{1,0:T(8,128)(2,1)S(1)}, u32[]{:S(2)}, u32[]{:S(2)}) collective-permute-start(bf16[64,256]{1,0:T(8,128)(2,1)S(1)} %fusion), channel_id=1, source_target_pairs={{0,8},{2,10},{4,12},{6,14},{8,0},{10,2},{12,4},{14,6},{16,24},{18,... | collective-permute-start | bytes 98312 | tf_op jit(solution)/shard_map/ppermute | solution.py:309
  11.3 7.3 %collective-permute-start.5 = (bf16[256,256]{1,0:T(8,128)(2,1)S(1)}, bf16[256,256]{1,0:T(8,128)(2,1)S(1)}, u32[]{:S(2)}, u32[]{:S(2)}) collective-permute-start(bf16[256,256]{1,0:T(8,128)(2,1)S(1)} %pad_maximum_fusion.line_ref), channel_id=1, source_target_pairs={{0,6},{2,4},{4,2},{6,0},{8,14},{10,12},{12,10},{14,8},{16,22},{18,... | collective-permute-start | bytes 393224 | tf_op jit(solution)/shard_map/ppermute | solution.py:309
  13.8 5.6 %collective-permute-start.4 = (bf16[256,256]{1,0:T(8,128)(2,1)S(1)}, bf16[256,256]{1,0:T(8,128)(2,1)S(1)}, u32[]{:S(2)}, u32[]{:S(2)}) collective-permute-start(bf16[256,256]{1,0:T(8,128)(2,1)S(1)} %pad_maximum_fusion.line_ref), channel_id=1, source_target_pairs={{0,4},{2,6},{4,0},{6,2},{8,12},{10,14},{12,8},{14,10},{16,20},{18,... | collective-permute-start | bytes 393224 | tf_op jit(solution)/shard_map/ppermute | solution.py:309
  14.3 5.1 %collective-permute-start.3 = (bf16[256,256]{1,0:T(8,128)(2,1)S(1)}, bf16[256,256]{1,0:T(8,128)(2,1)S(1)}, u32[]{:S(2)}, u32[]{:S(2)}) collective-permute-start(bf16[256,256]{1,0:T(8,128)(2,1)S(1)} %pad_maximum_fusion.line_ref), channel_id=1, source_target_pairs={{0,2},{2,0},{4,6},{6,4},{8,10},{10,8},{12,14},{14,12},{16,18},{18,... | collective-permute-start | bytes 393224 | tf_op jit(solution)/shard_map/ppermute | solution.py:309
  14.8 0.9 %copy-start = (bf16[128,1024]{1,0:T(8,128)(2,1)S(1)}, bf16[128,1024]{1,0:T(8,128)(2,1)}, u32[]{:S(2)}) copy-start(bf16[128,1024]{1,0:T(8,128)(2,1)} %q_hbm.1) | copy-start | bytes 786436
  15.8 0.9 %copy-start.1 = (bf16[128,1024]{1,0:T(8,128)(2,1)S(1)}, bf16[128,1024]{1,0:T(8,128)(2,1)}, u32[]{:S(2)}) copy-start(bf16[128,1024]{1,0:T(8,128)(2,1)} %g_hbm.1) | copy-start | bytes 786436
  16.7 0.7 %copy-start.2 = (s32[8]{0:T(128)S(1)}, s32[8]{0:T(128)}, u32[]{:S(2)}) copy-start(s32[8]{0:T(128)} %lengths_ref.1) | copy-start | bytes 100
  18.3 1.6 %collective-permute-start.6 = (bf16[256,256]{1,0:T(8,128)(2,1)S(1)}, bf16[256,256]{1,0:T(8,128)(2,1)S(1)}, u32[]{:S(2)}, u32[]{:S(2)}) collective-permute-start(bf16[256,256]{1,0:T(8,128)(2,1)S(1)} %get-tuple-element.24.refs_0_), channel_id=1, source_target_pairs={{0,1},{1,0},{2,3},{3,2},{4,5},{5,4},{6,7},{7,6},{8,9},{9,8},{10,11... | collective-permute-start | bytes 393224 | tf_op jit(solution)/shard_map/ppermute | solution.py:309
  18.6 1.3 %collective-permute-start.9 = (bf16[256,256]{1,0:T(8,128)(2,1)S(1)}, bf16[256,256]{1,0:T(8,128)(2,1)S(1)}, u32[]{:S(2)}, u32[]{:S(2)}) collective-permute-start(bf16[256,256]{1,0:T(8,128)(2,1)S(1)} %collective-permute-done.5.refs_3_), channel_id=1, source_target_pairs={{0,1},{1,0},{2,3},{3,2},{4,5},{5,4},{6,7},{7,6},{8,9},{9,8},{10,11... | collective-permute-start | bytes 393224 | tf_op jit(solution)/shard_map/ppermute | solution.py:309
  19.4 1.3 %collective-permute-start.8 = (bf16[256,256]{1,0:T(8,128)(2,1)S(1)}, bf16[256,256]{1,0:T(8,128)(2,1)S(1)}, u32[]{:S(2)}, u32[]{:S(2)}) collective-permute-start(bf16[256,256]{1,0:T(8,128)(2,1)S(1)} %collective-permute-done.4.refs_2_), channel_id=1, source_target_pairs={{0,1},{1,0},{2,3},{3,2},{4,5},{5,4},{6,7},{7,6},{8,9},{9,8},{10,11... | collective-permute-start | bytes 393224 | tf_op jit(solution)/shard_map/ppermute | solution.py:309
  19.4 1.5 %collective-permute-start.7 = (bf16[256,256]{1,0:T(8,128)(2,1)S(1)}, bf16[256,256]{1,0:T(8,128)(2,1)S(1)}, u32[]{:S(2)}, u32[]{:S(2)}) collective-permute-start(bf16[256,256]{1,0:T(8,128)(2,1)S(1)} %collective-permute-done.3.refs_1_), channel_id=1, source_target_pairs={{0,1},{1,0},{2,3},{3,2},{4,5},{5,4},{6,7},{7,6},{8,9},{9,8},{10,11... | collective-permute-start | bytes 393224 | tf_op jit(solution)/shard_map/ppermute | solution.py:309
  23.5 1.4 %collective-permute-start.11 = (bf16[256,256]{1,0:T(8,128)(2,1)S(1)}, bf16[256,256]{1,0:T(8,128)(2,1)S(1)}, u32[]{:S(2)}, u32[]{:S(2)}) collective-permute-start(bf16[256,256]{1,0:T(8,128)(2,1)S(1)} %get-tuple-element.32), channel_id=1, source_target_pairs={{0,1},{1,0},{2,3},{3,2},{4,5},{5,4},{6,7},{7,6},{8,9},{9,8},{10,11... | collective-permute-start | bytes 393224 | tf_op jit(solution)/shard_map/ppermute | solution.py:309
  23.9 4.8 %collective-permute-start.10 = (bf16[256,256]{1,0:T(8,128)(2,1)S(1)}, bf16[256,256]{1,0:T(8,128)(2,1)S(1)}, u32[]{:S(2)}, u32[]{:S(2)}) collective-permute-start(bf16[256,256]{1,0:T(8,128)(2,1)S(1)} %get-tuple-element.28), channel_id=1, source_target_pairs={{0,1},{1,0},{2,3},{3,2},{4,5},{5,4},{6,7},{7,6},{8,9},{9,8},{10,11... | collective-permute-start | bytes 393224 | tf_op jit(solution)/shard_map/ppermute | solution.py:309
  24.1 2.0 %collective-permute-start.13 = (bf16[256,256]{1,0:T(8,128)(2,1)S(1)}, bf16[256,256]{1,0:T(8,128)(2,1)S(1)}, u32[]{:S(2)}, u32[]{:S(2)}) collective-permute-start(bf16[256,256]{1,0:T(8,128)(2,1)S(1)} %get-tuple-element.34), channel_id=1, source_target_pairs={{0,1},{1,0},{2,3},{3,2},{4,5},{5,4},{6,7},{7,6},{8,9},{9,8},{10,11... | collective-permute-start | bytes 393224 | tf_op jit(solution)/shard_map/ppermute | solution.py:309
  24.5 3.2 %collective-permute-start.15 = (bf16[256,256]{1,0:T(8,128)(2,1)S(1)}, bf16[256,256]{1,0:T(8,128)(2,1)S(1)}, u32[]{:S(2)}, u32[]{:S(2)}) collective-permute-start(bf16[256,256]{1,0:T(8,128)(2,1)S(1)} %get-tuple-element.36), channel_id=1, source_target_pairs={{0,1},{1,0},{2,3},{3,2},{4,5},{5,4},{6,7},{7,6},{8,9},{9,8},{10,11... | collective-permute-start | bytes 393224 | tf_op jit(solution)/shard_map/ppermute | solution.py:309
  25.0 6.4 %collective-permute-start.12 = (bf16[256,256]{1,0:T(8,128)(2,1)S(1)}, bf16[256,256]{1,0:T(8,128)(2,1)S(1)}, u32[]{:S(2)}, u32[]{:S(2)}) collective-permute-start(bf16[256,256]{1,0:T(8,128)(2,1)S(1)} %add_convert_fusion.3), channel_id=1, source_target_pairs={{0,2},{2,0},{4,6},{6,4},{8,10},{10,8},{12,14},{14,12},{16,18},{18,... | collective-permute-start | bytes 393224 | tf_op jit(solution)/shard_map/ppermute | solution.py:309
  26.1 8.3 %collective-permute-start.14 = (bf16[256,256]{1,0:T(8,128)(2,1)S(1)}, bf16[256,256]{1,0:T(8,128)(2,1)S(1)}, u32[]{:S(2)}, u32[]{:S(2)}) collective-permute-start(bf16[256,256]{1,0:T(8,128)(2,1)S(1)} %add_convert_fusion.2), channel_id=1, source_target_pairs={{0,4},{2,6},{4,0},{6,2},{8,12},{10,14},{12,8},{14,10},{16,20},{18,... | collective-permute-start | bytes 393224 | tf_op jit(solution)/shard_map/ppermute | solution.py:309
  27.7 6.7 %collective-permute-start.16 = (bf16[256,256]{1,0:T(8,128)(2,1)S(1)}, bf16[256,256]{1,0:T(8,128)(2,1)S(1)}, u32[]{:S(2)}, u32[]{:S(2)}) collective-permute-start(bf16[256,256]{1,0:T(8,128)(2,1)S(1)} %add_convert_fusion.1), channel_id=1, source_target_pairs={{0,6},{2,4},{4,2},{6,0},{8,14},{10,12},{12,10},{14,8},{16,22},{18,... | collective-permute-start | bytes 393224 | tf_op jit(solution)/shard_map/ppermute | solution.py:309
  34.5 7.1 %collective-permute-start.17 = (bf16[64,256]{1,0:T(8,128)(2,1)S(1)}, bf16[64,256]{1,0:T(8,128)(2,1)S(1)}, u32[]{:S(2)}, u32[]{:S(2)}) collective-permute-start(bf16[64,256]{1,0:T(8,128)(2,1)S(1)} %get-tuple-element.37), channel_id=1, source_target_pairs={{0,8},{2,10},{4,12},{6,14},{8,0},{10,2},{12,4},{14,6},{16,24},{18,... | collective-permute-start | bytes 98312 | tf_op jit(solution)/shard_map/ppermute | solution.py:309
  35.3 7.9 %collective-permute-start.19 = (bf16[64,256]{1,0:T(8,128)(2,1)S(1)}, bf16[64,256]{1,0:T(8,128)(2,1)S(1)}, u32[]{:S(2)}, u32[]{:S(2)}) collective-permute-start(bf16[64,256]{1,0:T(8,128)(2,1)S(1)} %get-tuple-element.38), channel_id=1, source_target_pairs={{0,24},{2,26},{4,28},{6,30},{8,16},{10,18},{12,20},{14,22},{16,8},... | collective-permute-start | bytes 98312 | tf_op jit(solution)/shard_map/ppermute | solution.py:309
  41.1 4.8 %collective-permute-start.18 = (bf16[64,256]{1,0:T(8,128)(2,1)S(1)}, bf16[64,256]{1,0:T(8,128)(2,1)S(1)}, u32[]{:S(2)}, u32[]{:S(2)}) collective-permute-start(bf16[64,256]{1,0:T(8,128)(2,1)S(1)} %get-tuple-element.39), channel_id=1, source_target_pairs={{0,16},{2,18},{4,20},{6,22},{8,24},{10,26},{12,28},{14,30},{16,0},... | collective-permute-start | bytes 98312 | tf_op jit(solution)/shard_map/ppermute | solution.py:309
where the time goes:
time: 46.5 us; the launch traced here: 46.6 us
  starting transfers between devices  21.9 us (47%)
  waiting for transfers between devices  14.2 us (31%)
  Pallas kernels  5.5 us (12%)
  local copies, waits for them, and re-layouts  3.18 us (7%)
  other arithmetic  0.99 us (2%)
  between operations  0.72 us (2%)
    ppermute x20, starting transfers between devices, swap(): return lax.ppermute(value, axis, pairs)  21.9 us
    ppermute x20, waiting for transfers between devices, swap(): return lax.ppermute(value, axis, pairs)  14.2 us
    pallas_call x1, Pallas kernels, attend(): pl.pallas_call(functools.partial(attend_kernel, ctx_count, dp_count, inne...  2.62 us
    unnamed x6, local copies, waits for them, and re-layouts  2.55 us
    pallas_call x1, Pallas kernels, query_side(): pl.pallas_call(functools.partial(query_kernel, ctx_count, tile), out_shap...  1.96 us
  transfers between devices with their start and end apart: 20, of which 12 were waited for; matrix products, arithmetic and copies ran while one was open for 0% of the time, Pallas kernels for 6%

commit v1 on v0

--- a/solution.py
+++ b/solution.py
@@ -29,7 +29,7 @@
 def prepare_kernel(
     ctx_count,
     tile,
-    lengths_ref,
+    lengths_hbm,
     q_hbm,
     g_hbm,
     line_ref,
@@ -37,8 +37,10 @@
     flip_ref,
     starts_ref,
     tiles_ref,
+    zero_ref,
     same_ref,
     raw_ref,
+    lengths_ref,
     sems,
 ):
     tok_rows = q_hbm.shape[0]
@@ -51,9 +53,13 @@
     ]
     for copy in copies:
         copy.start()
+    lengths_copy = pltpu.make_async_copy(lengths_hbm, lengths_ref, sems.at[2])
+    lengths_copy.start()
     same_ref[...] = line_ref[...]
+    zero_ref[...] = jnp.zeros_like(zero_ref)
     lane = lax.broadcasted_iota(jnp.int32, tiles_ref.shape, 1)
     tiles = jnp.zeros(tiles_ref.shape, jnp.int32)
+    lengths_copy.wait()
     for half in range(2):
         first = span_first(half, ctx_count, span_rows)
         query_pos = first + lax.rem(
@@ -83,17 +89,15 @@
 
 
 def attend_kernel(
-    ctx_count, dp_count, inner, tile, tiles_ref, starts_ref, stack_ref, flip_ref, *refs
+    ctx_count, dp_count, inner, tile, tiles_ref, starts_ref, stack_ref, flip_ref, _, *refs
 ):
     outer = ctx_count // inner
     piece_count = dp_count * inner
     kv_refs = refs[:piece_count]
     refs = refs[piece_count:]
-    keys_ref, dlogits_ref = refs[:2]
-    dkv_refs = refs[2 : piece_count + 2]
-    values_ref, acc_ref, terms_ref, dweights_ref, tops_ref, counts_ref, sem = refs[
-        piece_count + 2 :
-    ]
+    keys_ref, dlogits_ref, acc_ref = refs[:3]
+    dkv_refs = refs[3 : piece_count + 3]
+    values_ref, terms_ref, dweights_ref, tops_ref, counts_ref, sem = refs[piece_count + 3 :]
     cols, head_width = stack_ref.shape[2:]
     tok_rows = (keys_ref.shape[0] - tile) // ctx_count
     part_rows = tok_rows // dp_count
@@ -110,25 +114,28 @@
                 owner = ctx_index ^ (piece % inner) ^ (block * inner)
                 first = (dp_index ^ (piece // inner)) * part_rows
                 position = row_position(owner, first, ctx_count, part_rows, span_rows)
+                row = 2 * block * part_rows
                 yield (
                     piece,
-                    pl.ds(block * part_rows, part_rows),
+                    pl.ds(row, part_rows),
+                    pl.ds(row + part_rows, part_rows),
                     pl.ds(tile + position, part_rows),
                 )
 
     dead = jnp.zeros((tile, head_width), jnp.bfloat16)
     keys_ref[:tile, :] = dead
     values_ref[:tile, :] = dead
-    for piece, here, ordered in blocks():
-        keys_ref[ordered, :] = kv_refs[piece][here, :head_width]
-        values_ref[ordered, :] = kv_refs[piece][here, head_width:]
-    acc_ref[...] = jnp.zeros_like(acc_ref)
+    for piece, key_rows, value_rows, ordered in blocks():
+        keys_ref[ordered, :] = kv_refs[piece][key_rows, :]
+        values_ref[ordered, :] = kv_refs[piece][value_rows, :]
     count_copy.wait()
+    group = min(256, cols)
+    groups = [slice(start, start + group) for start in range(0, cols, group)]
 
     for half in range(2):
         first = span_first(half, ctx_count, span_rows)
         query_pos = first + lax.rem(
-            lax.broadcasted_iota(jnp.int32, (1, cols), 1), jnp.int32(span_rows)
+            lax.broadcasted_iota(jnp.int32, (1, group), 1), jnp.int32(span_rows)
         )
         doc_start = starts_ref[half]
         count = counts_ref[0, half]
@@ -139,33 +146,46 @@
             return position, rows, pl.ds(pl.multiple_of(index * tile, tile), tile)
 
         def sums_step(index, state):
-            top, total, mixed = state
             position, rows, slot = tile_rows(index)
-            logits = jnp.dot(
-                keys_ref[rows, :], flip_ref[half, 0], preferred_element_type=jnp.float32
-            )
-            key_pos = lax.broadcasted_iota(jnp.int32, (tile, cols), 0)
-            live = (key_pos >= doc_start - position) & (key_pos <= query_pos - position)
-            logits = jnp.where(live, logits * (scale * math.log2(math.e)), masked_value)
-            new_top = jnp.maximum(top, jnp.max(logits, axis=0, keepdims=True))
-            terms = jnp.exp2(logits - new_top)
-            dweights = jnp.dot(
-                values_ref[rows, :], flip_ref[half, 1], preferred_element_type=jnp.float32
-            )
-            terms_ref[slot, :] = terms
-            dweights_ref[slot, :] = dweights
-            tops_ref[pl.ds(index, 1), :] = new_top
-            decay = jnp.exp2(top - new_top)
-            return (
-                new_top,
-                total * decay + jnp.sum(terms, axis=0, keepdims=True),
-                mixed * decay + jnp.sum(terms * dweights, axis=0, keepdims=True),
-            )
-
-        zero = jnp.zeros((1, cols), jnp.float32)
-        top, total, mixed = lax.fori_loop(
-            0, count, sums_step, (jnp.full_like(zero, masked_value), zero, zero)
-        )
+            key_block, value_block = keys_ref[rows, :], values_ref[rows, :]
+            all_logits = [
+                jnp.dot(key_block, flip_ref[half, 0, :, lanes], preferred_element_type=jnp.float32)
+                for lanes in groups
+            ]
+            all_dweights = [
+                jnp.dot(
+                    value_block, flip_ref[half, 1, :, lanes], preferred_element_type=jnp.float32
+                )
+                for lanes in groups
+            ]
+            following = []
+            for lanes, logits, dweights, (top, total, mixed) in zip(
+                groups, all_logits, all_dweights, state
+            ):
+                key_pos = lax.broadcasted_iota(jnp.int32, logits.shape, 0)
+                live = (key_pos >= doc_start[:, lanes] - position) & (
+                    key_pos <= query_pos - position
+                )
+                logits = jnp.where(live, logits * (scale * math.log2(math.e)), masked_value)
+                new_top = jnp.maximum(top, jnp.max(logits, axis=0, keepdims=True))
+                terms = jnp.exp2(logits - new_top)
+                terms_ref[slot, lanes] = terms
+                dweights_ref[slot, lanes] = dweights
+                tops_ref[pl.ds(index, 1), lanes] = new_top
+                decay = jnp.exp2(top - new_top)
+                following.append(
+                    (
+                        new_top,
+                        total * decay + jnp.sum(terms, axis=0, keepdims=True),
+                        mixed * decay + jnp.sum(terms * dweights, axis=0, keepdims=True),
+                    )
+                )
+            return tuple(following)
+
+        zero = jnp.zeros((1, group), jnp.float32)
+        empty = (jnp.full_like(zero, masked_value), zero, zero)
+        sums = lax.fori_loop(0, count, sums_step, (empty,) * len(groups))
+        top, total, mixed = (jnp.concatenate(part, axis=1) for part in zip(*sums))
         inverse = 1.0 / total
         delta = mixed * inverse
 
@@ -174,7 +194,10 @@
             factor = jnp.exp2(tops_ref[pl.ds(index, 1), :] - top) * inverse
             weights = terms_ref[slot, :] * factor
             dlogits = (weights * (dweights_ref[slot, :] - delta)).astype(jnp.bfloat16)
-            dlogits_ref[half, slot, :] = dlogits
+            for lane_block in range(cols // head_width):
+                dlogits_ref[half, lane_block, slot, :] = dlogits[
+                    :, lane_block * head_width : (lane_block + 1) * head_width
+                ]
             acc_ref[1, rows, :] += jnp.dot(
                 weights.astype(jnp.bfloat16),
                 stack_ref[half, 1],
@@ -187,9 +210,9 @@
 
         lax.fori_loop(0, count, grads_step, 0)
 
-    for piece, here, ordered in blocks():
-        dkv_refs[piece][here, :head_width] = (scale * acc_ref[0, ordered, :]).astype(jnp.bfloat16)
-        dkv_refs[piece][here, head_width:] = acc_ref[1, ordered, :].astype(jnp.bfloat16)
+    for piece, key_rows, value_rows, ordered in blocks():
+        dkv_refs[piece][key_rows, :] = (scale * acc_ref[0, ordered, :]).astype(jnp.bfloat16)
+        dkv_refs[piece][value_rows, :] = acc_ref[1, ordered, :].astype(jnp.bfloat16)
 
 
 def query_kernel(
@@ -220,8 +243,11 @@
         def query_step(index, carry):
             rows = pl.ds(pl.multiple_of(end - index * tile, span_rows), tile)
             slot = pl.ds(pl.multiple_of(index * tile, tile), tile)
+            dlogits = jnp.concatenate(
+                [dlogits_ref[half, block, slot, :] for block in range(dlogits_ref.shape[1])], axis=1
+            )
             sum_ref[...] += jnp.dot(
-                keys_ref[rows, :].T, dlogits_ref[half, slot, :], preferred_element_type=jnp.float32
+                keys_ref[rows, :].T, dlogits, preferred_element_type=jnp.float32
             )
             return carry
 
@@ -236,6 +262,10 @@
 def prepare(ctx_count, tile, doc_lengths, queries, out_grads, head_width, line):
     tok_rows, width = queries.shape
     cols = width // head_width * (tok_rows // 2)
+    unmoved = [
+        pltpu.with_memory_space_constraint(argument, pltpu.HBM)
+        for argument in (doc_lengths, queries, out_grads)
+    ]
     return pl.pallas_call(
         functools.partial(prepare_kernel, ctx_count, tile),
         out_shape=(
@@ -243,48 +273,53 @@
             jax.ShapeDtypeStruct((2, 2, head_width, cols), jnp.bfloat16),
             jax.ShapeDtypeStruct((2, 1, cols), jnp.int32),
             jax.ShapeDtypeStruct((8, 128), jnp.int32),
+            jax.ShapeDtypeStruct((2, tile + ctx_count * tok_rows, head_width), jnp.float32),
             jax.ShapeDtypeStruct(line.shape, line.dtype),
         ),
-        in_specs=[smem, hbm, hbm, vmem],
-        out_specs=[vmem] * 5,
+        in_specs=[hbm, hbm, hbm, vmem],
+        out_specs=[vmem] * 6,
         scratch_shapes=[
             pltpu.VMEM((2, tok_rows, width), jnp.bfloat16),
-            pltpu.SemaphoreType.DMA((2,)),
+            pltpu.SMEM(doc_lengths.shape, jnp.int32),
+            pltpu.SemaphoreType.DMA((3,)),
         ],
         compiler_params=pltpu.CompilerParams(vmem_limit_bytes=4 * 1024 * 1024),
-    )(doc_lengths, queries, out_grads, line)
-
-
-def attend(ctx_count, dp_count, inner, tile, tiles, starts, stacked, flipped, pieces):
+    )(*unmoved, line)
+
+
+def attend(ctx_count, dp_count, inner, tile, tiles, starts, stacked, flipped, zeros, pieces):
     cols, head_width = stacked.shape[2:]
-    seq = dp_count * inner * pieces[0].shape[0]
+    seq = dp_count * inner * pieces[0].shape[0] // 2
     slots = -(-seq // tile)
     results = pl.pallas_call(
         functools.partial(attend_kernel, ctx_count, dp_count, inner, tile),
         out_shape=[
             jax.ShapeDtypeStruct((tile + seq, head_width), jnp.bfloat16),
-            jax.ShapeDtypeStruct((2, slots * tile, cols), jnp.bfloat16),
+            jax.ShapeDtypeStruct(
+                (2, cols // head_width, slots * tile, head_width), jnp.bfloat16
+            ),
+            jax.ShapeDtypeStruct(zeros.shape, zeros.dtype),
         ]
         + [jax.ShapeDtypeStruct(piece.shape, jnp.bfloat16) for piece in pieces],
-        in_specs=[vmem] * (4 + len(pieces)),
-        out_specs=[vmem] * (2 + len(pieces)),
+        in_specs=[vmem] * (5 + len(pieces)),
+        out_specs=[vmem] * (3 + len(pieces)),
         scratch_shapes=[
             pltpu.VMEM((tile + seq, head_width), jnp.bfloat16),
-            pltpu.VMEM((2, tile + seq, head_width), jnp.float32),
             pltpu.VMEM((slots * tile, cols), jnp.float32),
             pltpu.VMEM((slots * tile, cols), jnp.float32),
             pltpu.VMEM((slots, cols), jnp.float32),
             pltpu.SMEM((8, 128), jnp.int32),
             pltpu.SemaphoreType.DMA,
         ],
+        input_output_aliases={4: 2},
         compiler_params=pltpu.CompilerParams(vmem_limit_bytes=32 * 1024 * 1024),
-    )(tiles, starts, stacked, flipped, *pieces)
-    return results[0], results[1], results[2:]
+    )(tiles, starts, stacked, flipped, zeros, *pieces)
+    return results[0], results[1], results[3:]
 
 
 def query_side(ctx_count, tile, tiles, keys_ordered, dlogits, passed, tok_rows):
-    cols = dlogits.shape[2]
     head_width = keys_ordered.shape[1]
+    cols = dlogits.shape[1] * head_width
     return pl.pallas_call(
         functools.partial(query_kernel, ctx_count, tile),
         out_shape=(
@@ -321,21 +356,27 @@
     tok_rows, head_width = keys.shape
     part_rows = tok_rows // dp_count
     tile = math.gcd(256, ctx_count * tok_rows)
-    own = lax.dynamic_slice_in_dim(
-        jnp.concatenate([keys, values], axis=1), lax.axis_index("dp") * part_rows, part_rows, 0
+    start = lax.axis_index("dp") * part_rows
+    own_keys = lax.dynamic_slice_in_dim(keys, start, part_rows, 0)
+    own_values = lax.dynamic_slice_in_dim(values, start, part_rows, 0)
+    zero = jnp.zeros((), keys.dtype)
+    own = jnp.where(
+        lax.broadcasted_iota(jnp.int32, (2 * part_rows, head_width), 0) < part_rows,
+        lax.pad(own_keys, zero, ((0, part_rows, 0), (0, 0, 0))),
+        lax.pad(own_values, zero, ((part_rows, 0, 0), (0, 0, 0))),
     )
     line = jnp.concatenate(
         [own] + [swap(own, "ctx", block * inner) for block in range(1, outer)], axis=0
     )
     plane = [line] + [swap(line, "ctx", offset) for offset in range(1, inner)]
-    stacked, flipped, starts, tiles, plane[0] = prepare(
+    stacked, flipped, starts, tiles, zeros, plane[0] = prepare(
         ctx_count, tile, doc_lengths, queries, out_grads, head_width, line
     )
     pieces = plane + [
         swap(piece, "dp", offset) for offset in range(1, dp_count) for piece in plane
     ]
     keys_ordered, dlogits, parts = attend(
-        ctx_count, dp_count, inner, tile, tiles, starts, stacked, flipped, pieces
+        ctx_count, dp_count, inner, tile, tiles, starts, stacked, flipped, zeros, pieces
     )
     plane_sums = [
         total_of(
@@ -354,7 +395,7 @@
     kv_grads = total_of(
         [blocks[0]] + [swap(blocks[block], "ctx", block * inner) for block in range(1, outer)]
     )
-    return (query_grads, kv_grads[:, :head_width], kv_grads[:, head_width:])
+    return (query_grads, kv_grads[:part_rows], kv_grads[part_rows:])
 
 
 def solution(mesh):

time: 46.5 us -> 45.8 us (0.985)
  waiting for transfers between devices: 14.2 us -> 17.8 us
  starting transfers between devices: 21.9 us -> 19.7 us
  local copies, waits for them, and re-layouts: 3.18 us -> 1.37 us
  other arithmetic: 0.99 us -> 0.35 us
    ppermute x20, waiting for transfers between devices: 14.2 us -> 17.8 us  [swap(): return lax.ppermute(value, axis, pairs)]
    unnamed x6 -> x0, local copies, waits for them, and re-layouts: 2.55 us -> none
    ppermute x20, starting transfers between devices: 21.9 us -> 19.7 us  [swap(): return lax.ppermute(value, axis, pairs)]
    concatenate x1 -> x0, other arithmetic: 0.74 us -> none  [body(): jnp.concatenate([keys, values], axis=1)]
    dynamic_slice x0 -> x1, local copies, waits for them, and re-layouts: none -> 0.74 us  [body(): own_values = lax.dynamic_slice_in_dim(values, start, part_rows, 0)]
  transfers between devices with their start and end apart: 20 -> 20, of which waited for: 12 -> 11; matrix products, arithmetic and copies ran while one was open for 0% -> 0% of each run, Pallas kernels for 6% -> 7%
where the time goes in v1:
time: 45.8 us; the launch traced here: 45.4 us
  starting transfers between devices  19.7 us (43%)
  waiting for transfers between devices  17.8 us (39%)
  Pallas kernels  5.5 us (12%)
  local copies, waits for them, and re-layouts  1.37 us (3%)
  between operations  0.75 us (2%)
    ppermute x20, starting transfers between devices, swap(): return lax.ppermute(value, axis, pairs)  19.7 us
    ppermute x20, waiting for transfers between devices, swap(): return lax.ppermute(value, axis, pairs)  17.8 us
    pallas_call x1, Pallas kernels, attend(): pl.pallas_call(functools.partial(attend_kernel, ctx_count, dp_count, inne...  2.28 us
    pallas_call x1, Pallas kernels, query_side(): pl.pallas_call(functools.partial(query_kernel, ctx_count, tile), out_shap...  1.97 us
    pallas_call x1, Pallas kernels, prepare(): pl.pallas_call(functools.partial(prepare_kernel, ctx_count, tile), out_sh...  1.26 us
  transfers between devices with their start and end apart: 20, of which 11 were waited for; matrix products, arithmetic and copies ran while one was open for 0% of the time, Pallas kernels for 7%

profile of v1, /device:TPU:0, one launch (start us, length us, event | category | flops | bytes accessed | tf_op | source)
XLA Modules:
  0.0 45.4 jit_solution(16906450138142806879)
XLA Ops:
  0.6 0.7 %constant_dynamic-slice_fusion = (bf16[64,128]{1,0:T(8,128)(2,1)S(1)}, bf16[64,128]{1,0:T(8,128)(2,1)S(1)}) fusion(bf16[128,128]{1,0:T(8,128)(2,1)} %param.7, s32[]{:T(128)S(6)} %select_n.8, bf16[128,128]{1,0:T(8,128)(2,1)} %param.6), kind=kLoop, calls=%fused_computation.8 | loop fusion | bytes 65540 | tf_op jit(solution)/shard_map/dynamic_slice | solution.py:361
  1.5 5.1 %collective-permute-start.2 = (bf16[128,128]{1,0:T(8,128)(2,1)S(1)}, bf16[128,128]{1,0:T(8,128)(2,1)S(1)}, u32[]{:S(2)}, u32[]{:S(2)}) collective-permute-start(bf16[128,128]{1,0:T(8,128)(2,1)S(1)} %pad_select_fusion), channel_id=1, source_target_pairs={{0,24},{2,26},{4,28},{6,30},{8,16},{10,18},{12,20},{14,22},{16,8},... | collective-permute-start | bytes 98312 | tf_op jit(solution)/shard_map/ppermute | solution.py:344
  6.6 0.6 %collective-permute-start = (bf16[128,128]{1,0:T(8,128)(2,1)S(1)}, bf16[128,128]{1,0:T(8,128)(2,1)S(1)}, u32[]{:S(2)}, u32[]{:S(2)}) collective-permute-start(bf16[128,128]{1,0:T(8,128)(2,1)S(1)} %pad_select_fusion), channel_id=1, source_target_pairs={{0,8},{2,10},{4,12},{6,14},{8,0},{10,2},{12,4},{14,6},{16,24},{18,... | collective-permute-start | bytes 98312 | tf_op jit(solution)/shard_map/ppermute | solution.py:344
  7.2 1.3 %collective-permute-done.2 = bf16[128,128]{1,0:T(8,128)(2,1)S(1)} collective-permute-done((bf16[128,128]{1,0:T(8,128)(2,1)S(1)}, bf16[128,128]{1,0:T(8,128)(2,1)S(1)}, u32[]{:S(2)}, u32[]{:S(2)}) %collective-permute-start.2) | collective-permute-done | bytes 32800 | tf_op jit(solution)/shard_map/ppermute | solution.py:344
  8.5 2.9 %collective-permute-done.1 = bf16[128,128]{1,0:T(8,128)(2,1)S(1)} collective-permute-done((bf16[128,128]{1,0:T(8,128)(2,1)S(1)}, bf16[128,128]{1,0:T(8,128)(2,1)S(1)}, u32[]{:S(2)}, u32[]{:S(2)}) %collective-permute-start.1) | collective-permute-done | bytes 32800 | tf_op jit(solution)/shard_map/ppermute | solution.py:344
  11.4 2.5 %collective-permute-start.5 = (bf16[512,128]{1,0:T(8,128)(2,1)S(1)}, bf16[512,128]{1,0:T(8,128)(2,1)S(1)}, u32[]{:S(2)}, u32[]{:S(2)}) collective-permute-start(bf16[512,128]{1,0:T(8,128)(2,1)S(1)} %pad_maximum_fusion.line_ref), channel_id=1, source_target_pairs={{0,6},{2,4},{4,2},{6,0},{8,14},{10,12},{12,10},{14,8},{16,22},{18,... | collective-permute-start | bytes 393224 | tf_op jit(solution)/shard_map/ppermute | solution.py:344
  13.9 0.5 %collective-permute-start.4 = (bf16[512,128]{1,0:T(8,128)(2,1)S(1)}, bf16[512,128]{1,0:T(8,128)(2,1)S(1)}, u32[]{:S(2)}, u32[]{:S(2)}) collective-permute-start(bf16[512,128]{1,0:T(8,128)(2,1)S(1)} %pad_maximum_fusion.line_ref), channel_id=1, source_target_pairs={{0,4},{2,6},{4,0},{6,2},{8,12},{10,14},{12,8},{14,10},{16,20},{18,... | collective-permute-start | bytes 393224 | tf_op jit(solution)/shard_map/ppermute | solution.py:344
  14.5 0.5 %collective-permute-start.3 = (bf16[512,128]{1,0:T(8,128)(2,1)S(1)}, bf16[512,128]{1,0:T(8,128)(2,1)S(1)}, u32[]{:S(2)}, u32[]{:S(2)}) collective-permute-start(bf16[512,128]{1,0:T(8,128)(2,1)S(1)} %pad_maximum_fusion.line_ref), channel_id=1, source_target_pairs={{0,2},{2,0},{4,6},{6,4},{8,10},{10,8},{12,14},{14,12},{16,18},{18,... | collective-permute-start | bytes 393224 | tf_op jit(solution)/shard_map/ppermute | solution.py:344
  15.0 1.3 %shard_map.76 = (bf16[2,2,512,128]{3,2,1,0:T(8,128)(2,1)S(1)}, bf16[2,2,128,512]{3,2,1,0:T(8,128)(2,1)S(1)}, s32[2,1,512]{2,1,0:T(1,128)S(1)}, s32[8,128]{1,0:T(...) custom-call(s32[8]{0:T(128)} %lengths_hbm.1, bf16[128,1024]{1,0:T(8,128)(2,1)} %q_hbm.1, ...), custom_call_target="tpu_custom_call" | custom-call | tf_op jit(solution)/shard_map/pallas_call | solution.py:269
  16.3 2.4 %collective-permute-done.5.refs_3_ = bf16[512,128]{1,0:T(8,128)(2,1)S(1)} collective-permute-done((bf16[512,128]{1,0:T(8,128)(2,1)S(1)}, bf16[512,128]{1,0:T(8,128)(2,1)S(1)}, u32[]{:S(2)}, u32[]{:S(2)}) %collective-permute-start.5) | collective-permute-done | bytes 131104 | tf_op jit(solution)/shard_map/ppermute | solution.py:344
  18.8 0.8 %collective-permute-done.4.refs_2_ = bf16[512,128]{1,0:T(8,128)(2,1)S(1)} collective-permute-done((bf16[512,128]{1,0:T(8,128)(2,1)S(1)}, bf16[512,128]{1,0:T(8,128)(2,1)S(1)}, u32[]{:S(2)}, u32[]{:S(2)}) %collective-permute-start.4) | collective-permute-done | bytes 131104 | tf_op jit(solution)/shard_map/ppermute | solution.py:344
  19.6 0.5 %collective-permute-start.7 = (bf16[512,128]{1,0:T(8,128)(2,1)S(1)}, bf16[512,128]{1,0:T(8,128)(2,1)S(1)}, u32[]{:S(2)}, u32[]{:S(2)}) collective-permute-start(bf16[512,128]{1,0:T(8,128)(2,1)S(1)} %collective-permute-done.3.refs_1_), channel_id=1, source_target_pairs={{0,1},{1,0},{2,3},{3,2},{4,5},{5,4},{6,7},{7,6},{8,9},{9,8},{10,11... | collective-permute-start | bytes 393224 | tf_op jit(solution)/shard_map/ppermute | solution.py:344
  20.1 0.8 %collective-permute-done.8.refs_6_ = bf16[512,128]{1,0:T(8,128)(2,1)S(1)} collective-permute-done((bf16[512,128]{1,0:T(8,128)(2,1)S(1)}, bf16[512,128]{1,0:T(8,128)(2,1)S(1)}, u32[]{:S(2)}, u32[]{:S(2)}) %collective-permute-start.8) | collective-permute-done | bytes 131104 | tf_op jit(solution)/shard_map/ppermute | solution.py:344
  21.1 2.3 %shard_map.77 = (bf16[2304,128]{1,0:T(8,128)(2,1)S(1)}, bf16[2,4,2048,128]{3,2,1,0:T(8,128)(2,1)S(1)}, f32[2,2304,128]{2,1,0:T(8,128)S(1)}, bf16[512,128]{1,0:T(...) custom-call(s32[8,128]{1,0:T(8,128)S(1)} %get-tuple-element.21.tiles, ...), custom_call_target="tpu_custom_call", output_to_operand_aliasing={{2}: (4, {})} | custom-call | tf_op jit(solution)/shard_map/pallas_call | solution.py:294
  23.4 0.4 collective-permute-start.11
  24.8 1.8 %collective-permute-start.12 = (bf16[512,128]{1,0:T(8,128)(2,1)S(1)}, bf16[512,128]{1,0:T(8,128)(2,1)S(1)}, u32[]{:S(2)}, u32[]{:S(2)}) collective-permute-start(bf16[512,128]{1,0:T(8,128)(2,1)S(1)} %add_convert_fusion.3), channel_id=1, source_target_pairs={{0,2},{2,0},{4,6},{6,4},{8,10},{10,8},{12,14},{14,12},{16,18},{18,... | collective-permute-start | bytes 393224 | tf_op jit(solution)/shard_map/ppermute | solution.py:344
  26.9 1.8 %collective-permute-start.16 = (bf16[512,128]{1,0:T(8,128)(2,1)S(1)}, bf16[512,128]{1,0:T(8,128)(2,1)S(1)}, u32[]{:S(2)}, u32[]{:S(2)}) collective-permute-start(bf16[512,128]{1,0:T(8,128)(2,1)S(1)} %add_convert_fusion.1), channel_id=1, source_target_pairs={{0,6},{2,4},{4,2},{6,0},{8,14},{10,12},{12,10},{14,8},{16,22},{18,... | collective-permute-start | bytes 393224 | tf_op jit(solution)/shard_map/ppermute | solution.py:344
  28.7 2.0 %shard_map.78 = (bf16[128,1024]{1,0:T(8,128)(2,1)}, bf16[512,128]{1,0:T(8,128)(2,1)S(1)}) custom-call(s32[8,128]{1,0:T(8,128)S(1)} %get-tuple-element.21.tiles_ref, bf16[2304,128]{1,0:T(8,128)(2,1)S(1)} %get-tuple-element.27.keys_ref, bf16[2,4,2048,128]{3,2,1,0:T(8,128)(2,1)S(1)} %get-tuple-element.28.dlogits_ref, ...), custom_call_target="tpu_custom_call" | custom-call | tf_op jit(solution)/shard_map/pallas_call | solution.py:323
  30.7 4.2 %collective-permute-done.14 = bf16[512,128]{1,0:T(8,128)(2,1)S(1)} collective-permute-done((bf16[512,128]{1,0:T(8,128)(2,1)S(1)}, bf16[512,128]{1,0:T(8,128)(2,1)S(1)}, u32[]{:S(2)}, u32[]{:S(2)}) %collective-permute-start.14) | collective-permute-done | bytes 131104 | tf_op jit(solution)/shard_map/ppermute | solution.py:344
  35.1 2.2 %collective-permute-start.17 = (bf16[128,128]{1,0:T(8,128)(2,1)S(1)}, bf16[128,128]{1,0:T(8,128)(2,1)S(1)}, u32[]{:S(2)}, u32[]{:S(2)}) collective-permute-start(bf16[128,128]{1,0:T(8,128)(2,1)S(1)} %get-tuple-element.39), channel_id=1, source_target_pairs={{0,8},{2,10},{4,12},{6,14},{8,0},{10,2},{12,4},{14,6},{16,24},{18,... | collective-permute-start | bytes 98312 | tf_op jit(solution)/shard_map/ppermute | solution.py:344
  37.2 2.8 %collective-permute-start.19 = (bf16[128,128]{1,0:T(8,128)(2,1)S(1)}, bf16[128,128]{1,0:T(8,128)(2,1)S(1)}, u32[]{:S(2)}, u32[]{:S(2)}) collective-permute-start(bf16[128,128]{1,0:T(8,128)(2,1)S(1)} %get-tuple-element.40), channel_id=1, source_target_pairs={{0,24},{2,26},{4,28},{6,30},{8,16},{10,18},{12,20},{14,22},{16,8},... | collective-permute-start | bytes 98312 | tf_op jit(solution)/shard_map/ppermute | solution.py:344
  40.0 2.9 %collective-permute-done.19 = bf16[128,128]{1,0:T(8,128)(2,1)S(1)} collective-permute-done((bf16[128,128]{1,0:T(8,128)(2,1)S(1)}, bf16[128,128]{1,0:T(8,128)(2,1)S(1)}, u32[]{:S(2)}, u32[]{:S(2)}) %collective-permute-start.19) | collective-permute-done | bytes 32800 | tf_op jit(solution)/shard_map/ppermute | solution.py:344
  42.9 1.9 %collective-permute-done.18 = bf16[128,128]{1,0:T(8,128)(2,1)S(1)} collective-permute-done((bf16[128,128]{1,0:T(8,128)(2,1)S(1)}, bf16[128,128]{1,0:T(8,128)(2,1)S(1)}, u32[]{:S(2)}, u32[]{:S(2)}) %collective-permute-start.18) | collective-permute-done | bytes 32800 | tf_op jit(solution)/shard_map/ppermute | solution.py:344
  44.8 0.6 %fusion.1 = (bf16[64,128]{1,0:T(8,128)(2,1)}, bf16[64,128]{1,0:T(8,128)(2,1)}) fusion(bf16[128,128]{1,0:T(8,128)(2,1)S(1)} %add_convert_fusion.5), kind=kLoop, calls=%fused_computation.12 | loop fusion | bytes 65536 | tf_op jit(solution)/shard_map/slice | solution.py:398
  (31 shorter events, 1.9 us)
Async XLA Ops:
  1.5 7.0 %collective-permute-start.2 = (bf16[128,128]{1,0:T(8,128)(2,1)S(1)}, bf16[128,128]{1,0:T(8,128)(2,1)S(1)}, u32[]{:S(2)}, u32[]{:S(2)}) collective-permute-start(bf16[128,128]{1,0:T(8,128)(2,1)S(1)} %pad_select_fusion), channel_id=1, source_target_pairs={{0,24},{2,26},{4,28},{6,30},{8,16},{10,18},{12,20},{14,22},{16,8},... | collective-permute-start | bytes 98312 | tf_op jit(solution)/shard_map/ppermute | solution.py:344
  6.6 4.8 %collective-permute-start.1 = (bf16[128,128]{1,0:T(8,128)(2,1)S(1)}, bf16[128,128]{1,0:T(8,128)(2,1)S(1)}, u32[]{:S(2)}, u32[]{:S(2)}) collective-permute-start(bf16[128,128]{1,0:T(8,128)(2,1)S(1)} %pad_select_fusion), channel_id=1, source_target_pairs={{0,16},{2,18},{4,20},{6,22},{8,24},{10,26},{12,28},{14,30},{16,0},... | collective-permute-start | bytes 98312 | tf_op jit(solution)/shard_map/ppermute | solution.py:344
  6.6 4.8 %collective-permute-start = (bf16[128,128]{1,0:T(8,128)(2,1)S(1)}, bf16[128,128]{1,0:T(8,128)(2,1)S(1)}, u32[]{:S(2)}, u32[]{:S(2)}) collective-permute-start(bf16[128,128]{1,0:T(8,128)(2,1)S(1)} %pad_select_fusion), channel_id=1, source_target_pairs={{0,8},{2,10},{4,12},{6,14},{8,0},{10,2},{12,4},{14,6},{16,24},{18,... | collective-permute-start | bytes 98312 | tf_op jit(solution)/shard_map/ppermute | solution.py:344
  11.4 7.3 %collective-permute-start.5 = (bf16[512,128]{1,0:T(8,128)(2,1)S(1)}, bf16[512,128]{1,0:T(8,128)(2,1)S(1)}, u32[]{:S(2)}, u32[]{:S(2)}) collective-permute-start(bf16[512,128]{1,0:T(8,128)(2,1)S(1)} %pad_maximum_fusion.line_ref), channel_id=1, source_target_pairs={{0,6},{2,4},{4,2},{6,0},{8,14},{10,12},{12,10},{14,8},{16,22},{18,... | collective-permute-start | bytes 393224 | tf_op jit(solution)/shard_map/ppermute | solution.py:344
  13.9 5.6 %collective-permute-start.4 = (bf16[512,128]{1,0:T(8,128)(2,1)S(1)}, bf16[512,128]{1,0:T(8,128)(2,1)S(1)}, u32[]{:S(2)}, u32[]{:S(2)}) collective-permute-start(bf16[512,128]{1,0:T(8,128)(2,1)S(1)} %pad_maximum_fusion.line_ref), channel_id=1, source_target_pairs={{0,4},{2,6},{4,0},{6,2},{8,12},{10,14},{12,8},{14,10},{16,20},{18,... | collective-permute-start | bytes 393224 | tf_op jit(solution)/shard_map/ppermute | solution.py:344
  14.5 5.1 %collective-permute-start.3 = (bf16[512,128]{1,0:T(8,128)(2,1)S(1)}, bf16[512,128]{1,0:T(8,128)(2,1)S(1)}, u32[]{:S(2)}, u32[]{:S(2)}) collective-permute-start(bf16[512,128]{1,0:T(8,128)(2,1)S(1)} %pad_maximum_fusion.line_ref), channel_id=1, source_target_pairs={{0,2},{2,0},{4,6},{6,4},{8,10},{10,8},{12,14},{14,12},{16,18},{18,... | collective-permute-start | bytes 393224 | tf_op jit(solution)/shard_map/ppermute | solution.py:344
  16.3 3.8 %collective-permute-start.6 = (bf16[512,128]{1,0:T(8,128)(2,1)S(1)}, bf16[512,128]{1,0:T(8,128)(2,1)S(1)}, u32[]{:S(2)}, u32[]{:S(2)}) collective-permute-start(bf16[512,128]{1,0:T(8,128)(2,1)S(1)} %get-tuple-element.26.refs_0_), channel_id=1, source_target_pairs={{0,1},{1,0},{2,3},{3,2},{4,5},{5,4},{6,7},{7,6},{8,9},{9,8},{10,11... | collective-permute-start | bytes 393224 | tf_op jit(solution)/shard_map/ppermute | solution.py:344
  18.8 1.3 %collective-permute-start.9 = (bf16[512,128]{1,0:T(8,128)(2,1)S(1)}, bf16[512,128]{1,0:T(8,128)(2,1)S(1)}, u32[]{:S(2)}, u32[]{:S(2)}) collective-permute-start(bf16[512,128]{1,0:T(8,128)(2,1)S(1)} %collective-permute-done.5.refs_3_), channel_id=1, source_target_pairs={{0,1},{1,0},{2,3},{3,2},{4,5},{5,4},{6,7},{7,6},{8,9},{9,8},{10,11... | collective-permute-start | bytes 393224 | tf_op jit(solution)/shard_map/ppermute | solution.py:344
  19.5 1.3 %collective-permute-start.8 = (bf16[512,128]{1,0:T(8,128)(2,1)S(1)}, bf16[512,128]{1,0:T(8,128)(2,1)S(1)}, u32[]{:S(2)}, u32[]{:S(2)}) collective-permute-start(bf16[512,128]{1,0:T(8,128)(2,1)S(1)} %collective-permute-done.4.refs_2_), channel_id=1, source_target_pairs={{0,1},{1,0},{2,3},{3,2},{4,5},{5,4},{6,7},{7,6},{8,9},{9,8},{10,11... | collective-permute-start | bytes 393224 | tf_op jit(solution)/shard_map/ppermute | solution.py:344
  19.6 1.5 %collective-permute-start.7 = (bf16[512,128]{1,0:T(8,128)(2,1)S(1)}, bf16[512,128]{1,0:T(8,128)(2,1)S(1)}, u32[]{:S(2)}, u32[]{:S(2)}) collective-permute-start(bf16[512,128]{1,0:T(8,128)(2,1)S(1)} %collective-permute-done.3.refs_1_), channel_id=1, source_target_pairs={{0,1},{1,0},{2,3},{3,2},{4,5},{5,4},{6,7},{7,6},{8,9},{9,8},{10,11... | collective-permute-start | bytes 393224 | tf_op jit(solution)/shard_map/ppermute | solution.py:344
  23.4 1.4 %collective-permute-start.11 = (bf16[512,128]{1,0:T(8,128)(2,1)S(1)}, bf16[512,128]{1,0:T(8,128)(2,1)S(1)}, u32[]{:S(2)}, u32[]{:S(2)}) collective-permute-start(bf16[512,128]{1,0:T(8,128)(2,1)S(1)} %get-tuple-element.34), channel_id=1, source_target_pairs={{0,1},{1,0},{2,3},{3,2},{4,5},{5,4},{6,7},{7,6},{8,9},{9,8},{10,11... | collective-permute-start | bytes 393224 | tf_op jit(solution)/shard_map/ppermute | solution.py:344
  23.8 4.9 %collective-permute-start.10 = (bf16[512,128]{1,0:T(8,128)(2,1)S(1)}, bf16[512,128]{1,0:T(8,128)(2,1)S(1)}, u32[]{:S(2)}, u32[]{:S(2)}) collective-permute-start(bf16[512,128]{1,0:T(8,128)(2,1)S(1)} %get-tuple-element.30), channel_id=1, source_target_pairs={{0,1},{1,0},{2,3},{3,2},{4,5},{5,4},{6,7},{7,6},{8,9},{9,8},{10,11... | collective-permute-start | bytes 393224 | tf_op jit(solution)/shard_map/ppermute | solution.py:344
  23.9 2.7 %collective-permute-start.13 = (bf16[512,128]{1,0:T(8,128)(2,1)S(1)}, bf16[512,128]{1,0:T(8,128)(2,1)S(1)}, u32[]{:S(2)}, u32[]{:S(2)}) collective-permute-start(bf16[512,128]{1,0:T(8,128)(2,1)S(1)} %get-tuple-element.36), channel_id=1, source_target_pairs={{0,1},{1,0},{2,3},{3,2},{4,5},{5,4},{6,7},{7,6},{8,9},{9,8},{10,11... | collective-permute-start | bytes 393224 | tf_op jit(solution)/shard_map/ppermute | solution.py:344
  24.3 2.5 %collective-permute-start.15 = (bf16[512,128]{1,0:T(8,128)(2,1)S(1)}, bf16[512,128]{1,0:T(8,128)(2,1)S(1)}, u32[]{:S(2)}, u32[]{:S(2)}) collective-permute-start(bf16[512,128]{1,0:T(8,128)(2,1)S(1)} %get-tuple-element.38), channel_id=1, source_target_pairs={{0,1},{1,0},{2,3},{3,2},{4,5},{5,4},{6,7},{7,6},{8,9},{9,8},{10,11... | collective-permute-start | bytes 393224 | tf_op jit(solution)/shard_map/ppermute | solution.py:344
  24.8 5.9 %collective-permute-start.12 = (bf16[512,128]{1,0:T(8,128)(2,1)S(1)}, bf16[512,128]{1,0:T(8,128)(2,1)S(1)}, u32[]{:S(2)}, u32[]{:S(2)}) collective-permute-start(bf16[512,128]{1,0:T(8,128)(2,1)S(1)} %add_convert_fusion.3), channel_id=1, source_target_pairs={{0,2},{2,0},{4,6},{6,4},{8,10},{10,8},{12,14},{14,12},{16,18},{18,... | collective-permute-start | bytes 393224 | tf_op jit(solution)/shard_map/ppermute | solution.py:344
  26.6 8.3 %collective-permute-start.14 = (bf16[512,128]{1,0:T(8,128)(2,1)S(1)}, bf16[512,128]{1,0:T(8,128)(2,1)S(1)}, u32[]{:S(2)}, u32[]{:S(2)}) collective-permute-start(bf16[512,128]{1,0:T(8,128)(2,1)S(1)} %add_convert_fusion.2), channel_id=1, source_target_pairs={{0,4},{2,6},{4,0},{6,2},{8,12},{10,14},{12,8},{14,10},{16,20},{18,... | collective-permute-start | bytes 393224 | tf_op jit(solution)/shard_map/ppermute | solution.py:344
  26.9 8.1 %collective-permute-start.16 = (bf16[512,128]{1,0:T(8,128)(2,1)S(1)}, bf16[512,128]{1,0:T(8,128)(2,1)S(1)}, u32[]{:S(2)}, u32[]{:S(2)}) collective-permute-start(bf16[512,128]{1,0:T(8,128)(2,1)S(1)} %add_convert_fusion.1), channel_id=1, source_target_pairs={{0,6},{2,4},{4,2},{6,0},{8,14},{10,12},{12,10},{14,8},{16,22},{18,... | collective-permute-start | bytes 393224 | tf_op jit(solution)/shard_map/ppermute | solution.py:344
  35.1 4.9 %collective-permute-start.17 = (bf16[128,128]{1,0:T(8,128)(2,1)S(1)}, bf16[128,128]{1,0:T(8,128)(2,1)S(1)}, u32[]{:S(2)}, u32[]{:S(2)}) collective-permute-start(bf16[128,128]{1,0:T(8,128)(2,1)S(1)} %get-tuple-element.39), channel_id=1, source_target_pairs={{0,8},{2,10},{4,12},{6,14},{8,0},{10,2},{12,4},{14,6},{16,24},{18,... | collective-permute-start | bytes 98312 | tf_op jit(solution)/shard_map/ppermute | solution.py:344
  37.2 5.7 %collective-permute-start.19 = (bf16[128,128]{1,0:T(8,128)(2,1)S(1)}, bf16[128,128]{1,0:T(8,128)(2,1)S(1)}, u32[]{:S(2)}, u32[]{:S(2)}) collective-permute-start(bf16[128,128]{1,0:T(8,128)(2,1)S(1)} %get-tuple-element.40), channel_id=1, source_target_pairs={{0,24},{2,26},{4,28},{6,30},{8,16},{10,18},{12,20},{14,22},{16,8},... | collective-permute-start | bytes 98312 | tf_op jit(solution)/shard_map/ppermute | solution.py:344
  40.0 4.8 %collective-permute-start.18 = (bf16[128,128]{1,0:T(8,128)(2,1)S(1)}, bf16[128,128]{1,0:T(8,128)(2,1)S(1)}, u32[]{:S(2)}, u32[]{:S(2)}) collective-permute-start(bf16[128,128]{1,0:T(8,128)(2,1)S(1)} %get-tuple-element.41), channel_id=1, source_target_pairs={{0,16},{2,18},{4,20},{6,22},{8,24},{10,26},{12,28},{14,30},{16,0},... | collective-permute-start | bytes 98312 | tf_op jit(solution)/shard_map/ppermute | solution.py:344
